TPU v7x, 256 devices: a whole 4x4x8 slice. The times are simulated.
256 devices in a mesh: section: 32 (over x, z_hi, y), tensor: 8 (over z_lo, core).
Axes of the slice: x: 4, y: 4, z: 8 (z_hi: 2, z_lo: 4; z = z_hi * 4 + z_lo), core: 2. Of those that a mesh axis runs over, the one named last changes fastest.
Arguments:
- down_terms: bfloat16 [32, 8, 128, 16384], P('section', 'tensor'), may hold values from -6 to 6
- residual: bfloat16 [32, 128, 16384], P('section', 'tensor'), may hold values from -6 to 6
- norm_gain: bfloat16 [32, 16384], P('section'), may hold values from 0.099609375 to 1.8984375
- kv_weight: bfloat16 [32, 16384, 2048], P('section', None, 'tensor'), may hold values from -0.046875 to 0.046875
Outputs:
- keys_values: bfloat16 [32, 128, 2048], P('section', None, 'tensor')
All inputs are finite; a program needn't handle non-finite values.
Results may differ from a plain program's by a relative error of at most 0.02.
Values may be sent and summed in bfloat16 or wider, within the bound.
A program may use at most 64 MiB of HBM per device.

v0:
```python
import jax
import jax.numpy as jnp
from jax import lax
from jax.sharding import PartitionSpec as P


def passed_along(array, axis, by):
    devices = lax.axis_size(axis)
    return lax.ppermute(array, axis, [(i, (i + by) % devices) for i in range(devices)])


def body(down_terms, residual, norm_gain, kv_weight):
    own_terms = down_terms[0, 0]
    stream_rows = residual[0]
    gain_row = norm_gain[0].astype(jnp.float32)
    kv_cols = kv_weight[0]
    mixed = lax.psum_scatter(
        own_terms.astype(jnp.float32).astype(jnp.bfloat16),
        "tensor",
        scatter_dimension=0,
        tiled=True,
    ).astype(jnp.float32)
    stream = stream_rows.astype(jnp.float32) + mixed
    scale = lax.rsqrt(jnp.mean(stream * stream, axis=1, keepdims=True) + 1e-05)
    normed = (stream * scale * gain_row[None, :]).astype(jnp.bfloat16)
    full_tokens = lax.all_gather(normed, "tensor", axis=0, tiled=True)
    arrived = passed_along(full_tokens, "section", 1)
    result = jnp.dot(arrived, kv_cols, preferred_element_type=jnp.float32)
    return result.astype(jnp.bfloat16)[None]


def solution(mesh):
    in_specs = (
        P("section", "tensor", None, None),
        P("section", "tensor", None),
        P("section", None),
        P("section", None, "tensor"),
    )
    out_specs = P("section", None, "tensor")
    return jax.shard_map(body, mesh=mesh, in_specs=in_specs, out_specs=out_specs, check_vma=False)
```

profile of v0, /device:TPU:1, one launch (start us, length us, event | category | flops | bytes accessed | tf_op | source)
XLA Modules:
  0.0 324.9 jit_solution(3903836302842944075)
XLA Ops:
  6.5 0.0 copy-start.1
  6.5 0.0 copy-start
  6.5 0.0 reduce-scatter.2.cloned.1.call-start
  6.5 0.7 reduce-scatter.2.cloned.1.call-update
  7.3 0.0 all-gather.2.cloned.1.call-start
  7.3 0.1 copy-done.1
  7.4 0.1 mul.31
  7.4 59.2 %reduce-scatter.2.cloned.1.call-done = bf16[16,16384]{1,0:T(8,128)(2,1)} async-done(((bf16[128,16384]{1,0:T(8,128)(2,1)}), bf16[16,16384]{1,0:T(8,128)(2,1)}) %reduce-scatter.2.cloned.1.call-update) | async-done | bytes 524304 | tf_op jit(solution)/shard_map/reduce_scatter | solution.py:17
  66.6 0.0 copy-done
  66.6 1.3 multiply_reduce_fusion
  68.0 2.0 multiply_convert_fusion
  70.0 0.0 all-gather.2.cloned.1.call-update
  70.0 53.7 %all-gather.2.cloned.1.call-done = bf16[128,16384]{1,0:T(8,128)(2,1)} async-done(((bf16[16,16384]{1,0:T(8,128)(2,1)}), bf16[128,16384]{1,0:T(8,128)(2,1)}) %all-gather.2.cloned.1.call-update) | async-done | bytes 4194320 | tf_op jit(solution)/shard_map/all_gather | solution.py:26
  123.7 1.2 collective-permute-start
  124.9 187.8 %collective-permute-done = bf16[128,16384]{1,0:T(8,128)(2,1)S(1)} collective-permute-done((bf16[128,16384]{1,0:T(8,128)(2,1)}, bf16[128,16384]{1,0:T(8,128)(2,1)S(1)}, u32[]{:S(2)}, u32[]{:S(2)}) %collective-permute-start) | collective-permute-done | bytes 4194336 | tf_op jit(solution)/shard_map/ppermute | solution.py:9
  312.8 5.3 %fusion.5 = bf16[1,128,256]{2,1,0:T(8,128)(2,1)} fusion(bf16[128,16384]{1,0:T(8,128)(2,1)S(1)} %collective-permute-done, bf16[1,16384,256]{2,1,0:T(8,128)(2,1)} %param.7), kind=kOutput, calls=%fused_computation.3 | convolution fusion | flops 1073774592 | bytes 12648448 | tf_op jit(solution)/shard_map/dot_general | solution.py:28
  (1 shorter events, 0.0 us)
Async XLA Ops:
  6.5 0.8 copy-start.1
  6.5 60.1 %copy-start = (bf16[1,16,16384]{2,1,0:T(8,128)(2,1)S(1)}, bf16[1,16,16384]{2,1,0:T(8,128)(2,1)}, u32[]{:S(2)}) copy-start(bf16[1,16,16384]{2,1,0:T(8,128)(2,1)} %param.5) | copy-start | bytes 1572868
  6.5 60.1 %reduce-scatter.2.cloned.1.call-start = ((), (), s32[]{:S(2)}) async-start(), calls=%async_computation.1 | async-start | bytes 4718592 | tf_op jit(solution)/shard_map/reduce_scatter | solution.py:17
  7.3 116.5 %all-gather.2.cloned.1.call-start = ((), (), s32[]{:S(2)}) async-start(), calls=%async_computation.2 | async-start | bytes 4718592 | tf_op jit(solution)/shard_map/all_gather | solution.py:26
  123.7 189.0 %collective-permute-start = (bf16[128,16384]{1,0:T(8,128)(2,1)}, bf16[128,16384]{1,0:T(8,128)(2,1)S(1)}, u32[]{:S(2)}, u32[]{:S(2)}) collective-permute-start(bf16[128,16384]{1,0:T(8,128)(2,1)} %all-gather.2.cloned.1.call-done), channel_id=1, source_target_pairs={{0,8},{8,16},{16,24},{24,32},{32,40},{40,48},{48,56},{56,64},{64,7... | collective-permute-start | bytes 12582920 | tf_op jit(solution)/shard_map/ppermute | solution.py:9
Sparse Core Ops, SparseCore 0:
  9.9 56.6 reduce-scatter.1
  70.1 53.5 all-gather.1
where the time goes:
time: 326 us; the launch traced here: 325 us
  waiting for transfers between devices  301 us (92%)
  between operations  13.4 us (4%)
  matrix products  5.27 us (2%)
  other arithmetic  3.45 us (1%)
    ppermute x1, waiting for transfers between devices, passed_along(): lax.ppermute(array, axis, [(i, (i + by) % devices) for i in range(devices)])  188 us
    reduce_scatter x1, waiting for transfers between devices, body(): lax.psum_scatter(own_terms.astype(jnp.float32).astype(jnp.bfloat16), 'ten...  59.2 us
    all_gather x1, waiting for transfers between devices, body(): full_tokens = lax.all_gather(normed, 'tensor', axis=0, tiled=True)  53.7 us
  transfers between devices with their start and end apart: 3, of which 3 were waited for; matrix products, arithmetic and copies ran while one was open for 0% of the time, Pallas kernels for 0%

commit v1 on v0

--- a/solution.py
+++ b/solution.py
@@ -23,8 +23,8 @@
     stream = stream_rows.astype(jnp.float32) + mixed
     scale = lax.rsqrt(jnp.mean(stream * stream, axis=1, keepdims=True) + 1e-05)
     normed = (stream * scale * gain_row[None, :]).astype(jnp.bfloat16)
-    full_tokens = lax.all_gather(normed, "tensor", axis=0, tiled=True)
-    arrived = passed_along(full_tokens, "section", 1)
+    hopped = passed_along(normed, "section", 1)
+    arrived = lax.all_gather(hopped, "tensor", axis=0, tiled=True)
     result = jnp.dot(arrived, kv_cols, preferred_element_type=jnp.float32)
     return result.astype(jnp.bfloat16)[None]
 

time: 326 us -> 167 us (0.51)
  waiting for transfers between devices: 301 us -> 141 us
    ppermute x1, waiting for transfers between devices: 188 us -> 22.6 us  [passed_along(): lax.ppermute(array, axis, [(i, (i + by) % devices) for i in range(devices)])]
    all_gather x1, waiting for transfers between devices: 53.7 us -> 58.2 us  [body(): arrived = lax.all_gather(hopped, 'tensor', axis=0, tiled=True)]
where the time goes in v1:
time: 167 us; the launch traced here: 166 us
  waiting for transfers between devices  141 us (84%)
  between operations  13.4 us (8%)
  matrix products  6.54 us (4%)
  other arithmetic  2.64 us (2%)
    reduce_scatter x1, waiting for transfers between devices, body(): lax.psum_scatter(own_terms.astype(jnp.float32).astype(jnp.bfloat16), 'ten...  59.2 us
    all_gather x1, waiting for transfers between devices, body(): arrived = lax.all_gather(hopped, 'tensor', axis=0, tiled=True)  58.2 us
    ppermute x1, waiting for transfers between devices, passed_along(): lax.ppermute(array, axis, [(i, (i + by) % devices) for i in range(devices)])  22.6 us
    dot_general x1, matrix products, body(): result = jnp.dot(arrived, kv_cols, preferred_element_type=jnp.float32)  6.54 us
  transfers between devices with their start and end apart: 3, of which 3 were waited for; matrix products, arithmetic and copies ran while one was open for 0% of the time, Pallas kernels for 0%

profile of v1, /device:TPU:1, one launch (start us, length us, event | category | flops | bytes accessed | tf_op | source)
XLA Modules:
  0.0 165.6 jit_solution(1222526563998898409)
XLA Ops:
  6.5 0.0 copy-start.2
  6.5 0.0 copy-start
  6.5 0.0 reduce-scatter.2.cloned.1.call-start
  6.5 0.7 reduce-scatter.2.cloned.1.call-update
  7.3 0.0 all-gather.2.cloned.1.call-start
  7.3 0.1 copy-done.2
  7.4 0.1 mul.31
  7.4 59.2 %reduce-scatter.2.cloned.1.call-done = bf16[16,16384]{1,0:T(8,128)(2,1)} async-done(((bf16[128,16384]{1,0:T(8,128)(2,1)}), bf16[16,16384]{1,0:T(8,128)(2,1)}) %reduce-scatter.2.cloned.1.call-update) | async-done | bytes 524304 | tf_op jit(solution)/shard_map/reduce_scatter | solution.py:17
  66.6 0.0 copy-done
  66.6 1.3 multiply_reduce_fusion
  68.0 1.2 multiply_convert_fusion
  69.2 1.3 collective-permute-start
  70.5 22.6 %collective-permute-done = bf16[16,16384]{1,0:T(8,128)(2,1)S(1)} collective-permute-done((bf16[16,16384]{1,0:T(8,128)(2,1)S(1)}, bf16[16,16384]{1,0:T(8,128)(2,1)S(1)}, u32[]{:S(2)}, u32[]{:S(2)}) %collective-permute-start) | collective-permute-done | bytes 524320 | tf_op jit(solution)/shard_map/ppermute | solution.py:9
  93.1 0.0 copy-start.1
  93.1 0.8 copy-done.1
  93.9 0.0 all-gather.2.cloned.1.call-update
  94.0 58.2 %all-gather.2.cloned.1.call-done = bf16[128,16384]{1,0:T(8,128)(2,1)} async-done(((bf16[16,16384]{1,0:T(8,128)(2,1)}), bf16[128,16384]{1,0:T(8,128)(2,1)}) %all-gather.2.cloned.1.call-update) | async-done | bytes 4194320 | tf_op jit(solution)/shard_map/all_gather | solution.py:27
  152.2 6.5 %fusion.5 = bf16[1,128,256]{2,1,0:T(8,128)(2,1)} fusion(bf16[128,16384]{1,0:T(8,128)(2,1)} %all-gather.2.cloned.1.call-done, bf16[1,16384,256]{2,1,0:T(8,128)(2,1)} %param.7), kind=kOutput, calls=%fused_computation.3 | convolution fusion | flops 1073774592 | bytes 12648448 | tf_op jit(solution)/shard_map/dot_general | solution.py:28
  (1 shorter events, 0.0 us)
Async XLA Ops:
  6.5 0.8 copy-start.2
  6.5 60.1 %copy-start = (bf16[1,16,16384]{2,1,0:T(8,128)(2,1)S(1)}, bf16[1,16,16384]{2,1,0:T(8,128)(2,1)}, u32[]{:S(2)}) copy-start(bf16[1,16,16384]{2,1,0:T(8,128)(2,1)} %param.5) | copy-start | bytes 1572868
  6.5 60.1 %reduce-scatter.2.cloned.1.call-start = ((), (), s32[]{:S(2)}) async-start(), calls=%async_computation.1 | async-start | bytes 4718592 | tf_op jit(solution)/shard_map/reduce_scatter | solution.py:17
  7.3 144.9 %all-gather.2.cloned.1.call-start = ((), (), s32[]{:S(2)}) async-start(), calls=%async_computation.2 | async-start | bytes 4718592 | tf_op jit(solution)/shard_map/all_gather | solution.py:27
  69.2 23.9 %collective-permute-start = (bf16[16,16384]{1,0:T(8,128)(2,1)S(1)}, bf16[16,16384]{1,0:T(8,128)(2,1)S(1)}, u32[]{:S(2)}, u32[]{:S(2)}) collective-permute-start(bf16[16,16384]{1,0:T(8,128)(2,1)S(1)} %multiply_convert_fusion), channel_id=1, source_target_pairs={{0,8},{8,16},{16,24},{24,32},{32,40},{40,48},{48,56},{56,64},{64,7... | collective-permute-start | bytes 1572872 | tf_op jit(solution)/shard_map/ppermute | solution.py:9
  93.1 0.8 copy-start.1
Sparse Core Ops, SparseCore 0:
  9.9 56.6 reduce-scatter.1
  94.1 58.0 all-gather.1

commit v2 on v1

v2 whole, which is shorter than its diff:
```python
import functools

import jax
import jax.numpy as jnp
from jax import lax
from jax.experimental import pallas as pl
from jax.experimental.pallas import tpu as pltpu
from jax.sharding import PartitionSpec as P

MESH = pl.DeviceIdType.MESH
BF16, F32 = jnp.bfloat16, jnp.float32

Y_RUN = 4
CHUNKS = 16
EDGE_SKEW = (0, 3, 4, 7, 8)
MID_SKEW = (1, 2, 5, 6, 8)


def kernel(n_section, down, res, gain, weight, out,
           own, pair, resv, gainv, wv, sent, got, x, scale_out, scales, acc, squares,
           own_sem, res_sem, gain_sem, w_sem, pair_recv, got_recv, x_recv, scale_recv, send_sem):
    chunks, _, rows, width = own.shape
    section, tensor = lax.axis_index("section"), lax.axis_index("tensor")
    z, core = tensor // 2, tensor % 2
    near = z // 2
    far = 1 - near
    is_edge = z % 3 == 0
    is_mid = z % 3 != 0
    inward = z + 1 - 2 * near
    outward = z - 1 + 2 * near
    flip_out = (section % Y_RUN) // (Y_RUN - 1)
    flip_in = 1 - (section % Y_RUN + Y_RUN - 1) // Y_RUN
    next_section = (section + 1) % n_section
    prev_section = (section + n_section - 1) % n_section
    next_near = (near + flip_out) % 2

    sibling_id = (section, z * 2 + 1 - core)
    inward_id = (section, inward * 2 + core)
    outward_id = (section, outward * 2 + core)
    next_id = (next_section, next_near * 6 + core)
    prev_id = (prev_section, ((near + flip_in) % 2) * 6 + core)

    def remote(src, dst, kind, recv, device):
        return pltpu.make_async_remote_copy(
            src_ref=src, dst_ref=dst, send_sem=send_sem.at[kind], recv_sem=recv, device_id=device, device_id_type=MESH
        )

    def cols(k):
        return pl.ds(pl.multiple_of(k * width, width), width)

    def own_copy(k):
        return pltpu.make_async_copy(down.at[:, core, :, cols(k)], own.at[k], own_sem.at[k])

    def res_copy(k):
        return pltpu.make_async_copy(res.at[:, cols(k)], resv.at[k], res_sem.at[k])

    def w_copy(k):
        return pltpu.make_async_copy(weight.at[cols(k)], wv.at[k], w_sem.at[k])

    def pair_copy(k):
        return remote(down.at[:, 1 - core, :, cols(k)], pair.at[k], 0, pair_recv.at[k], sibling_id)

    def got_copy(k, lane, kind, device):
        return remote(sent.at[lane, k], got.at[lane, k], kind, got_recv.at[lane, k], device)

    def part(of, flow):
        return pl.ds(of * 4 + flow * 2, 2)

    def hop_copy(k):
        return remote(sent.at[near, k], x.at[k, part(core, next_near)], 2, x_recv.at[core, next_near, k], next_id)

    def x_copy(k, of, flow, kind, device):
        return remote(x.at[k, part(of, flow)], x.at[k, part(of, flow)], kind, x_recv.at[of, flow, k], device)

    def scale_copy(of, flow, kind, device):
        return remote(scales.at[of, flow], scales.at[of, flow], kind, scale_recv.at[of, flow], device)

    gain_copy = pltpu.make_async_copy(gain, gainv, gain_sem)

    @pl.loop(0, chunks)
    def _(k):
        own_copy(k).start()

    gain_copy.start()

    barrier = pltpu.get_barrier_semaphore()

    def greet(device):
        pl.semaphore_signal(barrier, inc=1, device_id=device, device_id_type=MESH)

    greet(sibling_id)
    greet(inward_id)

    @pl.when(is_edge)
    def _():
        greet(next_id)
        greet(prev_id)
        pl.semaphore_wait(barrier, 4)

    @pl.when(is_mid)
    def _():
        greet(outward_id)
        pl.semaphore_wait(barrier, 3)

    @pl.loop(0, chunks)
    def _(k):
        pair_copy(k).start()

    @pl.loop(0, chunks)
    def _(k):
        res_copy(k).start()

    @pl.loop(0, chunks)
    def _(k):
        w_copy(k).start()

    acc[...] = jnp.zeros_like(acc)
    squares[...] = jnp.zeros_like(squares)
    gain_copy.wait()

    def partial_sum(k, lane, sub):
        index = lane * 2 + sub
        return own[k, index].astype(F32) + pair[k, index].astype(F32)

    def at(i, skew, body):
        k = i - skew

        @pl.when((k >= 0) & (k < chunks))
        def _():
            body(k)

    def arrived(k):
        own_copy(k).wait()
        pair_copy(k).wait_recv()

    def edge_far_reduce(k):
        arrived(k)
        for sub in range(2):
            sent[far, k, sub] = partial_sum(k, far, sub).astype(BF16)
        got_copy(k, far, 1, inward_id).start()

    def mid_far_reduce(k):
        arrived(k)
        got_copy(k, far, 1, inward_id).wait_recv()
        for sub in range(2):
            sent[far, k, sub] = (got[far, k, sub].astype(F32) + partial_sum(k, far, sub)).astype(BF16)
        got_copy(k, far, 1, inward_id).start()

    def near_sum(k, sub):
        mask = ((sub + z + 1) % 2).astype(F32)
        return got[near, k, sub].astype(F32) + partial_sum(k, near, sub) + resv[k].astype(F32) * mask

    def edge_near_reduce(k):
        res_copy(k).wait()
        got_copy(k, near, 1, inward_id).wait_recv()
        gain_row = gainv[:, cols(k)].astype(F32)
        for sub in range(2):
            stream = near_sum(k, sub)
            square = stream * stream
            folded = square[:, :128]
            for j in range(1, width // 128):
                folded = folded + square[:, j * 128:(j + 1) * 128]
            squares[sub] += folded
            sent[near, k, sub] = (stream * gain_row).astype(BF16)
        hop_copy(k).start()

        @pl.when(k == chunks - 1)
        def _():
            total = jnp.sum(squares[...], axis=2, keepdims=True) * (1.0 / (chunks * width))
            scale_out[...] = jnp.broadcast_to(lax.rsqrt(total + 1e-05), scale_out.shape)
            remote(scale_out, scales.at[core, next_near], 7, scale_recv.at[core, next_near], next_id).start()

    def mid_near_reduce(k):
        res_copy(k).wait()
        got_copy(k, near, 1, inward_id).wait_recv()
        for sub in range(2):
            sent[near, k, sub] = near_sum(k, sub).astype(BF16)
        got_copy(k, near, 2, outward_id).start()

    def near_spread(k):
        x_copy(k, core, near, 3, inward_id).wait_recv()
        x_copy(k, core, near, 3, inward_id).start()
        x_copy(k, core, near, 4, sibling_id).start()

        @pl.when(k == chunks - 1)
        def _():
            scale_copy(core, near, 8, inward_id).wait_recv()
            scale_copy(core, near, 8, inward_id).start()
            scale_copy(core, near, 9, sibling_id).start()

    def far_spread(k):
        x_copy(k, core, far, 6, sibling_id).wait_recv()

        @pl.when(is_mid)
        def _():
            x_copy(k, core, far, 5, outward_id).start()

        x_copy(k, core, far, 6, sibling_id).start()

        @pl.when(k == chunks - 1)
        def _():
            scale_copy(core, far, 11, sibling_id).wait_recv()

            @pl.when(is_mid)
            def _():
                scale_copy(core, far, 10, outward_id).start()

            scale_copy(core, far, 11, sibling_id).start()

    def product(k):
        w_copy(k).wait()
        for flow in range(2):
            x_copy(k, 1 - core, flow, 4, sibling_id).wait_recv()
        acc[...] += jnp.dot(x[k].reshape(8 * rows, width), wv[k], preferred_element_type=F32)

    @pl.when(is_edge)
    def _():
        @pl.loop(0, chunks + max(EDGE_SKEW))
        def _(i):
            at(i, EDGE_SKEW[0], edge_far_reduce)
            at(i, EDGE_SKEW[1], edge_near_reduce)
            at(i, EDGE_SKEW[2], near_spread)
            at(i, EDGE_SKEW[3], far_spread)
            at(i, EDGE_SKEW[4], product)

    @pl.when(is_mid)
    def _():
        @pl.loop(0, chunks + max(MID_SKEW))
        def _(i):
            at(i, MID_SKEW[0], mid_far_reduce)
            at(i, MID_SKEW[1], mid_near_reduce)
            at(i, MID_SKEW[2], near_spread)
            at(i, MID_SKEW[3], far_spread)
            at(i, MID_SKEW[4], product)

    for flow in range(2):
        scale_copy(1 - core, flow, 9, sibling_id).wait_recv()
    lane_of = (flip_in, 1 - flip_in)
    for of in range(2):
        for flow in range(2):
            for sub in range(2):
                start = (of * 4 + flow * 2 + sub) * rows
                factor = scales[of, flow, sub]
                block = acc[start:start + rows] * jnp.concatenate([factor, factor], axis=1)
                out[lane_of[flow] * 2 + sub, of] = block.astype(BF16)

    def sent_all(ref, kind):
        remote(ref, ref, kind, pair_recv.at[0], sibling_id).wait_send()

    sent_all(down.at[:, 1 - core], 0)
    sent_all(sent.at[far], 1)
    sent_all(sent.at[near], 2)
    sent_all(x.at[:, part(core, near)], 3)
    sent_all(x.at[:, part(core, near)], 4)
    sent_all(x.at[:, part(core, far)], 6)
    sent_all(scales.at[core, near], 8)
    sent_all(scales.at[core, near], 9)
    sent_all(scales.at[core, far], 11)

    @pl.when(is_edge)
    def _():
        sent_all(scale_out, 7)

    @pl.when(is_mid)
    def _():
        sent_all(x.at[:, part(core, far)], 5)
        sent_all(scales.at[core, far], 10)


def body(n_section, down_terms, residual, norm_gain, kv_weight):
    tokens, d = down_terms.shape[2:]
    kv = kv_weight.shape[2]
    rows, chunks = tokens // 8, CHUNKS
    width = d // chunks
    anywhere = pl.BlockSpec(memory_space=pl.ANY)
    out = pl.pallas_call(
        functools.partial(kernel, n_section),
        out_shape=jax.ShapeDtypeStruct((4, 2, rows, kv), BF16),
        in_specs=[anywhere] * 4,
        out_specs=pl.BlockSpec(memory_space=pltpu.VMEM),
        scratch_shapes=[
            pltpu.VMEM((chunks, 4, rows, width), BF16),
            pltpu.VMEM((chunks, 4, rows, width), BF16),
            pltpu.VMEM((chunks, rows, width), BF16),
            pltpu.VMEM((1, d), BF16),
            pltpu.VMEM((chunks, width, kv), BF16),
            pltpu.VMEM((2, chunks, 2, rows, width), BF16),
            pltpu.VMEM((2, chunks, 2, rows, width), BF16),
            pltpu.VMEM((chunks, 8, rows, width), BF16),
            pltpu.VMEM((2, rows, 128), F32),
            pltpu.VMEM((2, 2, 2, rows, 128), F32),
            pltpu.VMEM((tokens, kv), F32),
            pltpu.VMEM((2, rows, 128), F32),
            pltpu.SemaphoreType.DMA((chunks,)),
            pltpu.SemaphoreType.DMA((chunks,)),
            pltpu.SemaphoreType.DMA,
            pltpu.SemaphoreType.DMA((chunks,)),
            pltpu.SemaphoreType.DMA((chunks,)),
            pltpu.SemaphoreType.DMA((2, chunks)),
            pltpu.SemaphoreType.DMA((2, 2, chunks)),
            pltpu.SemaphoreType.DMA((2, 2)),
            pltpu.SemaphoreType.DMA((12,)),
        ],
        compiler_params=pltpu.CompilerParams(
            collective_id=0, has_side_effects=True, vmem_limit_bytes=48 * 1024 * 1024
        ),
        cost_estimate=pl.CostEstimate(flops=2 * tokens * d * kv, bytes_accessed=13 * 2**20, transcendentals=0),
    )(
        down_terms.reshape(4, 2, rows, d),
        residual.reshape(rows, d),
        norm_gain,
        kv_weight.reshape(d, kv),
    )
    return out.reshape(1, tokens, kv)


def solution(mesh):
    in_specs = (
        P("section", "tensor", None, None),
        P("section", "tensor", None),
        P("section", None),
        P("section", None, "tensor"),
    )
    out_specs = P("section", None, "tensor")
    return jax.shard_map(
        functools.partial(body, mesh.shape["section"]), mesh=mesh, in_specs=in_specs, out_specs=out_specs, check_vma=False
    )
```

time: 167 us -> 91.2 us (0.55)
  waiting for transfers between devices: 141 us -> 0 us
  Pallas kernels: 0 us -> 86.3 us
  between operations: 13.4 us -> 0.01 us
  matrix products: 6.54 us -> 0 us
  local copies, waits for them, and re-layouts: 0.89 us -> 4.7 us
  other arithmetic: 2.64 us -> 0 us
    pallas_call x0 -> x1, Pallas kernels: none -> 86.3 us  [body(): pl.pallas_call(functools.partial(kernel, n_section), out_shape=jax.ShapeD...]
    reduce_scatter x1 -> x0, waiting for transfers between devices: 59.2 us -> none  [body(): lax.psum_scatter(own_terms.astype(jnp.float32).astype(jnp.bfloat16), 'ten...]
    all_gather x1 -> x0, waiting for transfers between devices: 58.2 us -> none  [body(): arrived = lax.all_gather(hopped, 'tensor', axis=0, tiled=True)]
    ppermute x1 -> x0, waiting for transfers between devices: 22.6 us -> none  [passed_along(): lax.ppermute(array, axis, [(i, (i + by) % devices) for i in range(devices)])]
    dot_general x1 -> x0, matrix products: 6.54 us -> none  [body(): result = jnp.dot(arrived, kv_cols, preferred_element_type=jnp.float32)]
    unnamed x6 -> x7, local copies, waits for them, and re-layouts: 0.89 us -> 4.7 us
  transfers between devices with their start and end apart: 3 -> 0, of which waited for: 3 -> 0; matrix products, arithmetic and copies ran while one was open for 0% -> 0% of each run, Pallas kernels for 0% -> 0%
where the time goes in v2:
time: 91.2 us; the launch traced here: 91 us
  Pallas kernels  86.3 us (95%)
  local copies, waits for them, and re-layouts  4.7 us (5%)
    pallas_call x1, Pallas kernels, body(): pl.pallas_call(functools.partial(kernel, n_section), out_shape=jax.ShapeD...  86.3 us
    unnamed x7, local copies, waits for them, and re-layouts  4.7 us

profile of v2, /device:TPU:1, one launch (start us, length us, event | category | flops | bytes accessed | tf_op | source)
XLA Modules:
  0.0 91.0 jit_solution(692074766056431293)
XLA Ops:
  0.0 0.0 copy-start
  0.0 2.2 %copy-done = bf16[1,1,128,16384]{3,2,1,0:T(8,128)(2,1)S(1)} copy-done((bf16[1,1,128,16384]{3,2,1,0:T(8,128)(2,1)S(1)}, bf16[1,1,128,16384]{3,2,1,0:T(8,128)(2,1)}, u32[]{:S(2)}) %copy-start) | copy-done | bytes 4194328
  2.2 0.0 copy-start.1
  2.2 1.0 %copy-done.1 = bf16[1,16,16384]{2,1,0:T(8,128)(2,1)S(1)} copy-done((bf16[1,16,16384]{2,1,0:T(8,128)(2,1)S(1)}, bf16[1,16,16384]{2,1,0:T(8,128)(2,1)}, u32[]{:S(2)}) %copy-start.1) | copy-done | bytes 524312
  3.2 0.0 copy-start.2
  3.2 0.8 copy-done.2
  4.1 86.3 %shard_map.46 = bf16[4,2,16,256]{3,2,1,0:T(8,128)(2,1)S(1)} custom-call(bf16[4,2,16,16384]{3,2,1,0:T(8,128)(2,1)S(1)} %bitcast.4, bf16[16,16384]{1,0:T(8,128)(2,1)S(1)} %bitcast.5, bf16[1,16384]{1,0:T(2,128)(2,1)S(1)} %copy-done.2, bf16[16384,256]{1,0:T(8,128)(2,1)} %bitcast.7), custom_call_target="tpu_custom_call" | custom-call | flops 1073741824 | bytes 13631488 | tf_op jit(solution)/shard_map/pallas_call | solution.py:276
  90.4 0.6 copy.6
Async XLA Ops:
  0.0 2.2 %copy-start = (bf16[1,1,128,16384]{3,2,1,0:T(8,128)(2,1)S(1)}, bf16[1,1,128,16384]{3,2,1,0:T(8,128)(2,1)}, u32[]{:S(2)}) copy-start(bf16[1,1,128,16384]{3,2,1,0:T(8,128)(2,1)} %param.4) | copy-start | bytes 12582916
  2.2 1.0 %copy-start.1 = (bf16[1,16,16384]{2,1,0:T(8,128)(2,1)S(1)}, bf16[1,16,16384]{2,1,0:T(8,128)(2,1)}, u32[]{:S(2)}) copy-start(bf16[1,16,16384]{2,1,0:T(8,128)(2,1)} %param.5) | copy-start | bytes 1572868
  3.2 0.8 copy-start.2

commit v3 on v2

--- a/solution.py
+++ b/solution.py
@@ -12,13 +12,13 @@
 
 Y_RUN = 4
 CHUNKS = 16
-EDGE_SKEW = (0, 3, 4, 7, 8)
-MID_SKEW = (1, 2, 5, 6, 8)
+EDGE_SKEW = (0, 6, 14, 23, 26)
+MID_SKEW = (2, 4, 17, 20, 26)
 
 
 def kernel(n_section, down, res, gain, weight, out,
            own, pair, resv, gainv, wv, sent, got, x, scale_out, scales, acc, squares,
-           own_sem, res_sem, gain_sem, w_sem, pair_recv, got_recv, x_recv, scale_recv, send_sem):
+           own_sem, res_sem, gain_sem, w_sem, pair_recv, got_recv, x_recv, sibling_recv, scale_recv, send_sem, line_sem):
     chunks, _, rows, width = own.shape
     section, tensor = lax.axis_index("section"), lax.axis_index("tensor")
     z, core = tensor // 2, tensor % 2
@@ -67,15 +67,35 @@
         return pl.ds(of * 4 + flow * 2, 2)
 
     def hop_copy(k):
-        return remote(sent.at[near, k], x.at[k, part(core, next_near)], 2, x_recv.at[core, next_near, k], next_id)
+        return remote(sent.at[near, k], x.at[k, part(core, next_near)], 2, x_recv.at[next_near, k], next_id)
 
     def x_copy(k, of, flow, kind, device):
-        return remote(x.at[k, part(of, flow)], x.at[k, part(of, flow)], kind, x_recv.at[of, flow, k], device)
+        return remote(x.at[k, part(of, flow)], x.at[k, part(of, flow)], kind, x_recv.at[flow, k], device)
+
+    def both_copy(k):
+        mine = x.at[k, pl.ds(core * 4, 4)]
+        return remote(mine, mine, 4, sibling_recv.at[k], sibling_id)
 
     def scale_copy(of, flow, kind, device):
         return remote(scales.at[of, flow], scales.at[of, flow], kind, scale_recv.at[of, flow], device)
 
     gain_copy = pltpu.make_async_copy(gain, gainv, gain_sem)
+
+    barrier = pltpu.get_barrier_semaphore()
+
+    def greet(device):
+        pl.semaphore_signal(barrier, inc=1, device_id=device, device_id_type=MESH)
+
+    @pl.when(is_edge)
+    def _():
+        greet(inward_id)
+        greet((section, inward * 2 + 1 - core))
+        greet(prev_id)
+
+    @pl.when(is_mid)
+    def _():
+        greet(sibling_id)
+        greet(inward_id)
 
     @pl.loop(0, chunks)
     def _(k):
@@ -83,40 +103,25 @@
 
     gain_copy.start()
 
-    barrier = pltpu.get_barrier_semaphore()
-
-    def greet(device):
-        pl.semaphore_signal(barrier, inc=1, device_id=device, device_id_type=MESH)
-
-    greet(sibling_id)
-    greet(inward_id)
+    @pl.loop(0, chunks)
+    def _(k):
+        res_copy(k).start()
+
+    @pl.when(is_mid)
+    def _():
+        pl.semaphore_wait(barrier, 4)
+        pl.semaphore_signal(line_sem, inc=1, device_id=outward_id, device_id_type=MESH)
 
     @pl.when(is_edge)
     def _():
-        greet(next_id)
-        greet(prev_id)
-        pl.semaphore_wait(barrier, 4)
-
-    @pl.when(is_mid)
-    def _():
-        greet(outward_id)
-        pl.semaphore_wait(barrier, 3)
+        pl.semaphore_wait(line_sem, 1)
 
     @pl.loop(0, chunks)
     def _(k):
         pair_copy(k).start()
 
-    @pl.loop(0, chunks)
-    def _(k):
-        res_copy(k).start()
-
-    @pl.loop(0, chunks)
-    def _(k):
-        w_copy(k).start()
-
     acc[...] = jnp.zeros_like(acc)
     squares[...] = jnp.zeros_like(squares)
-    gain_copy.wait()
 
     def partial_sum(k, lane, sub):
         index = lane * 2 + sub
@@ -151,6 +156,12 @@
         return got[near, k, sub].astype(F32) + partial_sum(k, near, sub) + resv[k].astype(F32) * mask
 
     def edge_near_reduce(k):
+        w_copy(k).start()
+        @pl.when(k == 0)
+        def _():
+            gain_copy.wait()
+            pl.semaphore_wait(barrier, 1)
+
         res_copy(k).wait()
         got_copy(k, near, 1, inward_id).wait_recv()
         gain_row = gainv[:, cols(k)].astype(F32)
@@ -171,6 +182,11 @@
             remote(scale_out, scales.at[core, next_near], 7, scale_recv.at[core, next_near], next_id).start()
 
     def mid_near_reduce(k):
+        w_copy(k).start()
+        @pl.when(k == 0)
+        def _():
+            gain_copy.wait()
+
         res_copy(k).wait()
         got_copy(k, near, 1, inward_id).wait_recv()
         for sub in range(2):
@@ -180,7 +196,6 @@
     def near_spread(k):
         x_copy(k, core, near, 3, inward_id).wait_recv()
         x_copy(k, core, near, 3, inward_id).start()
-        x_copy(k, core, near, 4, sibling_id).start()
 
         @pl.when(k == chunks - 1)
         def _():
@@ -189,13 +204,13 @@
             scale_copy(core, near, 9, sibling_id).start()
 
     def far_spread(k):
-        x_copy(k, core, far, 6, sibling_id).wait_recv()
+        x_copy(k, core, far, 5, outward_id).wait_recv()
 
         @pl.when(is_mid)
         def _():
             x_copy(k, core, far, 5, outward_id).start()
 
-        x_copy(k, core, far, 6, sibling_id).start()
+        both_copy(k).start()
 
         @pl.when(k == chunks - 1)
         def _():
@@ -209,8 +224,7 @@
 
     def product(k):
         w_copy(k).wait()
-        for flow in range(2):
-            x_copy(k, 1 - core, flow, 4, sibling_id).wait_recv()
+        both_copy(k).wait_recv()
         acc[...] += jnp.dot(x[k].reshape(8 * rows, width), wv[k], preferred_element_type=F32)
 
     @pl.when(is_edge)
@@ -251,8 +265,7 @@
     sent_all(sent.at[far], 1)
     sent_all(sent.at[near], 2)
     sent_all(x.at[:, part(core, near)], 3)
-    sent_all(x.at[:, part(core, near)], 4)
-    sent_all(x.at[:, part(core, far)], 6)
+    sent_all(x.at[:, pl.ds(core * 4, 4)], 4)
     sent_all(scales.at[core, near], 8)
     sent_all(scales.at[core, near], 9)
     sent_all(scales.at[core, far], 11)
@@ -272,7 +285,7 @@
     kv = kv_weight.shape[2]
     rows, chunks = tokens // 8, CHUNKS
     width = d // chunks
-    anywhere = pl.BlockSpec(memory_space=pl.ANY)
+    anywhere = pl.BlockSpec(memory_space=pltpu.HBM)
     out = pl.pallas_call(
         functools.partial(kernel, n_section),
         out_shape=jax.ShapeDtypeStruct((4, 2, rows, kv), BF16),
@@ -297,12 +310,14 @@
             pltpu.SemaphoreType.DMA((chunks,)),
             pltpu.SemaphoreType.DMA((chunks,)),
             pltpu.SemaphoreType.DMA((2, chunks)),
-            pltpu.SemaphoreType.DMA((2, 2, chunks)),
+            pltpu.SemaphoreType.DMA((2, chunks)),
+            pltpu.SemaphoreType.DMA((chunks,)),
             pltpu.SemaphoreType.DMA((2, 2)),
             pltpu.SemaphoreType.DMA((12,)),
+            pltpu.SemaphoreType.REGULAR,
         ],
         compiler_params=pltpu.CompilerParams(
-            collective_id=0, has_side_effects=True, vmem_limit_bytes=48 * 1024 * 1024
+            collective_id=0, has_side_effects=True, vmem_limit_bytes=62 * 1024 * 1024
         ),
         cost_estimate=pl.CostEstimate(flops=2 * tokens * d * kv, bytes_accessed=13 * 2**20, transcendentals=0),
     )(

time: 91.2 us -> 68.6 us (0.75)
  Pallas kernels: 86.3 us -> 67 us
  local copies, waits for them, and re-layouts: 4.7 us -> 1.47 us
    pallas_call x1, Pallas kernels: 86.3 us -> 67 us  [body(): pl.pallas_call(functools.partial(kernel, n_section), out_shape=jax.ShapeD...]
    unnamed x7 -> x1, local copies, waits for them, and re-layouts: 4.7 us -> 1.47 us
where the time goes in v3:
time: 68.6 us; the launch traced here: 68.4 us
  Pallas kernels  67 us (98%)
  local copies, waits for them, and re-layouts  1.47 us (2%)
    pallas_call x1, Pallas kernels, body(): pl.pallas_call(functools.partial(kernel, n_section), out_shape=jax.ShapeD...  67 us
    unnamed x1, local copies, waits for them, and re-layouts  1.47 us

profile of v3, /device:TPU:1, one launch (start us, length us, event | category | flops | bytes accessed | tf_op | source)
XLA Modules:
  0.0 68.4 jit_solution(6419353081104724643)
XLA Ops:
  0.0 67.0 %shard_map.46 = bf16[4,2,16,256]{3,2,1,0:T(8,128)(2,1)} custom-call(bf16[4,2,16,16384]{3,2,1,0:T(8,128)(2,1)} %bitcast.5, bf16[16,16384]{1,0:T(8,128)(2,1)} %bitcast.6, bf16[1,16384]{1,0:T(2,128)(2,1)} %gain.1, bf16[16384,256]{1,0:T(8,128)(2,1)} %bitcast.4), custom_call_target="tpu_custom_call" | custom-call | flops 1073741824 | bytes 13631488 | tf_op jit(solution)/shard_map/pallas_call | solution.py:289
  67.0 1.5 %copy.6 = bf16[1,128,256]{2,1,0:T(8,128)(2,1)} copy(bf16[1,128,256]{2,1,0:T(8,128)(2,1)} %bitcast.7) | data formatting | bytes 131072

commit v4 on v3

--- a/solution.py
+++ b/solution.py
@@ -12,14 +12,14 @@
 
 Y_RUN = 4
 CHUNKS = 16
-EDGE_SKEW = (0, 6, 14, 23, 26)
-MID_SKEW = (2, 4, 17, 20, 26)
+EDGE_SKEW = (0, 6, 13, 23, 25)
+MID_SKEW = (2, 4, 17, 20, 25)
 
 
 def kernel(n_section, down, res, gain, weight, out,
            own, pair, resv, gainv, wv, sent, got, x, scale_out, scales, acc, squares,
-           own_sem, res_sem, gain_sem, w_sem, pair_recv, got_recv, x_recv, sibling_recv, scale_recv, send_sem, line_sem):
-    chunks, _, rows, width = own.shape
+           load_sem, pair_recv, got_recv, x_recv, sibling_recv, scale_recv, send_sem, line_sem):
+    chunks, _, rows, width = pair.shape
     section, tensor = lax.axis_index("section"), lax.axis_index("tensor")
     z, core = tensor // 2, tensor % 2
     near = z // 2
@@ -48,14 +48,10 @@
     def cols(k):
         return pl.ds(pl.multiple_of(k * width, width), width)
 
-    def own_copy(k):
-        return pltpu.make_async_copy(down.at[:, core, :, cols(k)], own.at[k], own_sem.at[k])
-
-    def res_copy(k):
-        return pltpu.make_async_copy(res.at[:, cols(k)], resv.at[k], res_sem.at[k])
-
-    def w_copy(k):
-        return pltpu.make_async_copy(weight.at[cols(k)], wv.at[k], w_sem.at[k])
+    own_copy = pltpu.make_async_copy(down.at[:, core], own, load_sem.at[0])
+    res_copy = pltpu.make_async_copy(res, resv, load_sem.at[1])
+    gain_copy = pltpu.make_async_copy(gain, gainv, load_sem.at[2])
+    w_copy = pltpu.make_async_copy(weight, wv, load_sem.at[3])
 
     def pair_copy(k):
         return remote(down.at[:, 1 - core, :, cols(k)], pair.at[k], 0, pair_recv.at[k], sibling_id)
@@ -79,8 +75,6 @@
     def scale_copy(of, flow, kind, device):
         return remote(scales.at[of, flow], scales.at[of, flow], kind, scale_recv.at[of, flow], device)
 
-    gain_copy = pltpu.make_async_copy(gain, gainv, gain_sem)
-
     barrier = pltpu.get_barrier_semaphore()
 
     def greet(device):
@@ -97,15 +91,9 @@
         greet(sibling_id)
         greet(inward_id)
 
-    @pl.loop(0, chunks)
-    def _(k):
-        own_copy(k).start()
-
+    own_copy.start()
+    res_copy.start()
     gain_copy.start()
-
-    @pl.loop(0, chunks)
-    def _(k):
-        res_copy(k).start()
 
     @pl.when(is_mid)
     def _():
@@ -120,12 +108,16 @@
     def _(k):
         pair_copy(k).start()
 
+    w_copy.start()
     acc[...] = jnp.zeros_like(acc)
     squares[...] = jnp.zeros_like(squares)
+    own_copy.wait()
+    res_copy.wait()
+    gain_copy.wait()
 
     def partial_sum(k, lane, sub):
         index = lane * 2 + sub
-        return own[k, index].astype(F32) + pair[k, index].astype(F32)
+        return own[index, :, cols(k)].astype(F32) + pair[k, index].astype(F32)
 
     def at(i, skew, body):
         k = i - skew
@@ -135,7 +127,6 @@
             body(k)
 
     def arrived(k):
-        own_copy(k).wait()
         pair_copy(k).wait_recv()
 
     def edge_far_reduce(k):
@@ -153,16 +144,13 @@
 
     def near_sum(k, sub):
         mask = ((sub + z + 1) % 2).astype(F32)
-        return got[near, k, sub].astype(F32) + partial_sum(k, near, sub) + resv[k].astype(F32) * mask
+        return got[near, k, sub].astype(F32) + partial_sum(k, near, sub) + resv[:, cols(k)].astype(F32) * mask
 
     def edge_near_reduce(k):
-        w_copy(k).start()
         @pl.when(k == 0)
         def _():
-            gain_copy.wait()
             pl.semaphore_wait(barrier, 1)
 
-        res_copy(k).wait()
         got_copy(k, near, 1, inward_id).wait_recv()
         gain_row = gainv[:, cols(k)].astype(F32)
         for sub in range(2):
@@ -182,12 +170,6 @@
             remote(scale_out, scales.at[core, next_near], 7, scale_recv.at[core, next_near], next_id).start()
 
     def mid_near_reduce(k):
-        w_copy(k).start()
-        @pl.when(k == 0)
-        def _():
-            gain_copy.wait()
-
-        res_copy(k).wait()
         got_copy(k, near, 1, inward_id).wait_recv()
         for sub in range(2):
             sent[near, k, sub] = near_sum(k, sub).astype(BF16)
@@ -223,15 +205,21 @@
             scale_copy(core, far, 11, sibling_id).start()
 
     def product(k):
-        w_copy(k).wait()
+        @pl.when(k == 0)
+        def _():
+            w_copy.wait()
+
         both_copy(k).wait_recv()
-        acc[...] += jnp.dot(x[k].reshape(8 * rows, width), wv[k], preferred_element_type=F32)
+        acc[...] += jnp.dot(x[k].reshape(8 * rows, width), wv[cols(k)], preferred_element_type=F32)
 
     @pl.when(is_edge)
     def _():
-        @pl.loop(0, chunks + max(EDGE_SKEW))
+        @pl.loop(0, chunks)
+        def _(k):
+            edge_far_reduce(k)
+
+        @pl.loop(min(EDGE_SKEW[1:]), chunks + max(EDGE_SKEW))
         def _(i):
-            at(i, EDGE_SKEW[0], edge_far_reduce)
             at(i, EDGE_SKEW[1], edge_near_reduce)
             at(i, EDGE_SKEW[2], near_spread)
             at(i, EDGE_SKEW[3], far_spread)
@@ -292,11 +280,11 @@
         in_specs=[anywhere] * 4,
         out_specs=pl.BlockSpec(memory_space=pltpu.VMEM),
         scratch_shapes=[
+            pltpu.VMEM((4, rows, d), BF16),
             pltpu.VMEM((chunks, 4, rows, width), BF16),
-            pltpu.VMEM((chunks, 4, rows, width), BF16),
-            pltpu.VMEM((chunks, rows, width), BF16),
+            pltpu.VMEM((rows, d), BF16),
             pltpu.VMEM((1, d), BF16),
-            pltpu.VMEM((chunks, width, kv), BF16),
+            pltpu.VMEM((d, kv), BF16),
             pltpu.VMEM((2, chunks, 2, rows, width), BF16),
             pltpu.VMEM((2, chunks, 2, rows, width), BF16),
             pltpu.VMEM((chunks, 8, rows, width), BF16),
@@ -304,10 +292,7 @@
             pltpu.VMEM((2, 2, 2, rows, 128), F32),
             pltpu.VMEM((tokens, kv), F32),
             pltpu.VMEM((2, rows, 128), F32),
-            pltpu.SemaphoreType.DMA((chunks,)),
-            pltpu.SemaphoreType.DMA((chunks,)),
-            pltpu.SemaphoreType.DMA,
-            pltpu.SemaphoreType.DMA((chunks,)),
+            pltpu.SemaphoreType.DMA((4,)),
             pltpu.SemaphoreType.DMA((chunks,)),
             pltpu.SemaphoreType.DMA((2, chunks)),
             pltpu.SemaphoreType.DMA((2, chunks)),

time: 68.6 us -> 66 us (0.962)
  Pallas kernels: 67 us -> 64.4 us
    pallas_call x1, Pallas kernels: 67 us -> 64.4 us  [body(): pl.pallas_call(functools.partial(kernel, n_section), out_shape=jax.ShapeD...]
where the time goes in v4:
time: 66 us; the launch traced here: 65.9 us
  Pallas kernels  64.4 us (98%)
  local copies, waits for them, and re-layouts  1.47 us (2%)
    pallas_call x1, Pallas kernels, body(): pl.pallas_call(functools.partial(kernel, n_section), out_shape=jax.ShapeD...  64.4 us
    unnamed x1, local copies, waits for them, and re-layouts  1.47 us

profile of v4, /device:TPU:1, one launch (start us, length us, event | category | flops | bytes accessed | tf_op | source)
XLA Modules:
  0.0 65.9 jit_solution(14126397185550560534)
XLA Ops:
  0.0 64.4 %shard_map.46 = bf16[4,2,16,256]{3,2,1,0:T(8,128)(2,1)} custom-call(bf16[4,2,16,16384]{3,2,1,0:T(8,128)(2,1)} %bitcast.5, bf16[16,16384]{1,0:T(8,128)(2,1)} %bitcast.6, bf16[1,16384]{1,0:T(2,128)(2,1)} %gain.1, bf16[16384,256]{1,0:T(8,128)(2,1)} %bitcast.4), custom_call_target="tpu_custom_call" | custom-call | flops 1073741824 | bytes 13631488 | tf_op jit(solution)/shard_map/pallas_call | solution.py:277
  64.4 1.5 %copy.6 = bf16[1,128,256]{2,1,0:T(8,128)(2,1)} copy(bf16[1,128,256]{2,1,0:T(8,128)(2,1)} %bitcast.7) | data formatting | bytes 131072

commit v5 on v4

--- a/solution.py
+++ b/solution.py
@@ -11,9 +11,9 @@
 BF16, F32 = jnp.bfloat16, jnp.float32
 
 Y_RUN = 4
-CHUNKS = 16
-EDGE_SKEW = (0, 6, 13, 23, 25)
-MID_SKEW = (2, 4, 17, 20, 25)
+CHUNKS = 32
+EDGE_SKEW = (0, 12, 28, 42, 44)
+MID_SKEW = (4, 8, 35, 40, 44)
 
 
 def kernel(n_section, down, res, gain, weight, out,
@@ -302,15 +302,13 @@
             pltpu.SemaphoreType.REGULAR,
         ],
         compiler_params=pltpu.CompilerParams(
-            collective_id=0, has_side_effects=True, vmem_limit_bytes=62 * 1024 * 1024
+            collective_id=0, has_side_effects=True, vmem_limit_bytes=40 * 1024 * 1024
         ),
         cost_estimate=pl.CostEstimate(flops=2 * tokens * d * kv, bytes_accessed=13 * 2**20, transcendentals=0),
-    )(
-        down_terms.reshape(4, 2, rows, d),
-        residual.reshape(rows, d),
-        norm_gain,
-        kv_weight.reshape(d, kv),
-    )
+    )(*(
+        pltpu.with_memory_space_constraint(array, pltpu.HBM)
+        for array in (down_terms.reshape(4, 2, rows, d), residual.reshape(rows, d), norm_gain, kv_weight.reshape(d, kv))
+    ))
     return out.reshape(1, tokens, kv)
 
 

time: 66 us -> 64.2 us (0.973)
  Pallas kernels: 64.4 us -> 63.4 us
  local copies, waits for them, and re-layouts: 1.47 us -> 0.63 us
    pallas_call x1, Pallas kernels: 64.4 us -> 63.4 us  [body(): pl.pallas_call(functools.partial(kernel, n_section), out_shape=jax.ShapeD...]
    unnamed x1, local copies, waits for them, and re-layouts: 1.47 us -> 0.63 us
where the time goes in v5:
time: 64.2 us; the launch traced here: 64.1 us
  Pallas kernels  63.4 us (99%)
    pallas_call x1, Pallas kernels, body(): pl.pallas_call(functools.partial(kernel, n_section), out_shape=jax.ShapeD...  63.4 us

profile of v5, /device:TPU:1, one launch (start us, length us, event | category | flops | bytes accessed | tf_op | source)
XLA Modules:
  0.0 64.1 jit_solution(6420151178067850816)
XLA Ops:
  0.0 63.4 %shard_map.46 = bf16[4,2,16,256]{3,2,1,0:T(8,128)(2,1)S(1)} custom-call(bf16[4,2,16,16384]{3,2,1,0:T(8,128)(2,1)} %bitcast.6, bf16[16,16384]{1,0:T(8,128)(2,1)} %bitcast.7, bf16[1,16384]{1,0:T(2,128)(2,1)} %gain.1, bf16[16384,256]{1,0:T(8,128)(2,1)} %bitcast.5), custom_call_target="tpu_custom_call" | custom-call | flops 1073741824 | bytes 13631488 | tf_op jit(solution)/shard_map/pallas_call | solution.py:277
  63.4 0.6 copy.6

commit v6 on v5

--- a/solution.py
+++ b/solution.py
@@ -186,7 +186,7 @@
             scale_copy(core, near, 9, sibling_id).start()
 
     def far_spread(k):
-        x_copy(k, core, far, 5, outward_id).wait_recv()
+        x_copy(k, core, far, 5, sibling_id).wait_recv()
 
         @pl.when(is_mid)
         def _():

time: 64.2 us -> 64.2 us (level)
  no operation moved by 1% of the time
where the time goes in v6:
time: 64.2 us; the launch traced here: 64.1 us
  Pallas kernels  63.4 us (99%)
    pallas_call x1, Pallas kernels, body(): pl.pallas_call(functools.partial(kernel, n_section), out_shape=jax.ShapeD...  63.4 us

profile of v6, /device:TPU:1, one launch (start us, length us, event | category | flops | bytes accessed | tf_op | source)
XLA Modules:
  0.0 64.1 jit_solution(13836770638351583238)
XLA Ops:
  0.0 63.4 %shard_map.46 = bf16[4,2,16,256]{3,2,1,0:T(8,128)(2,1)S(1)} custom-call(bf16[4,2,16,16384]{3,2,1,0:T(8,128)(2,1)} %bitcast.6, bf16[16,16384]{1,0:T(8,128)(2,1)} %bitcast.7, bf16[1,16384]{1,0:T(2,128)(2,1)} %gain.1, bf16[16384,256]{1,0:T(8,128)(2,1)} %bitcast.5), custom_call_target="tpu_custom_call" | custom-call | flops 1073741824 | bytes 13631488 | tf_op jit(solution)/shard_map/pallas_call | solution.py:277
  63.4 0.6 copy.6
